TPU v7x, 256 devices: a whole 4x4x8 slice. The times are simulated.
256 devices in a mesh: gz: 16 (over z, core), gy: 8 (over y, x_hi), orb: 2 (over x_lo).
Axes of the slice: x: 4 (x_hi: 2, x_lo: 2; x = x_hi * 2 + x_lo), y: 4, z: 8, core: 2. Of those that a mesh axis runs over, the one named last changes fastest.
Arguments:
- orbitals: bfloat16 [4096, 24, 576], P(('gz', 'gy', 'orb')), may hold values from -6 to 6
- occupation: float32 [4096], P(('gz', 'gy', 'orb')), may hold values from 0.5 to 2
- corners: int32 [4096, 3], P(('gz', 'gy', 'orb')), may hold values from 0 to 383, as said below
- kernel_widths: float32 [8], replicated, may hold values from 0.7 to 2.5
- w_in: float32 [8, 64], replicated, may hold values from -2 to 2
- b_in: float32 [64], replicated, may hold values from -3 to 3
- w_mid: float32 [64, 64], replicated, may hold values from -0.75 to 0.75
- b_mid: float32 [64], replicated, may hold values from -3 to 3
- w_out: float32 [64], replicated, may hold values from -0.75 to 0.75
- b_out: float32 [1], replicated, may hold values from -3 to 3
Outputs:
- potential: bfloat16 [384, 192, 128], P('gz', 'gy')
- applied: bfloat16 [4096, 24, 576], P(('gz', 'gy', 'orb'))
Inputs may be any that keep to these rules, and one draw needn't show every extreme that they name: Orbital i is held by device i // 16 of the axes gz, gy, orb taken together. Its row corners[i,1] lies in the 24 rows of that device's gy index. Among the 16 orbitals of one device, at most 2 have their plane corners[i,0] in the same slab of 24 planes, and on every device some slab holds exactly 2 of them. Columns lie in 0 to 127, rows in 0 to 191, planes in 0 to 383; the first and the last plane are taken in every draw.
All inputs are finite; a program needn't handle non-finite values.
Results may differ from a plain program's by a relative error of at most 0.0055.
Values may be sent and summed in bfloat16 or wider, within the bound.
No kernel may reach another device: no remote copies, remote signals or barrier semaphores. Data moves between devices by JAX's collectives and lax.ppermute only.
A program may use at most 64 MiB of HBM per device.

v0:
```python
import jax
import jax.numpy as jnp
from jax import lax
from jax.sharding import PartitionSpec as P

BOX = 24
CHAN = 8
RAD = 6
CZ = 24
CY = 24
NX = 128
CAP = 2
CELL_BLOCK = 12288
exact_mode = lax.Precision.HIGHEST


def shifted(x, axis, by):
    count = lax.axis_size(axis)
    return lax.ppermute(x, axis, [(i, (i + by) % count) for i in range(count)])


def extended_2(cells, sides, width):
    for axis, dim in sides:
        count = lax.axis_size(axis)
        head = lax.slice_in_dim(cells, 0, width, axis=dim)
        tail = lax.slice_in_dim(cells, cells.shape[dim] - width, cells.shape[dim], axis=dim)
        cells = jnp.concatenate(
            [
                lax.ppermute(tail, axis, [(i, (i + 1) % count) for i in range(count)]),
                cells,
                lax.ppermute(head, axis, [((i + 1) % count, i) for i in range(count)]),
            ],
            axis=dim,
        )
    return cells


def for_sending(x):
    return jax.tree.map(lambda a: a.astype(jnp.bfloat16) if a.dtype == jnp.float32 else a, x)


def kernel_taps(kernel_widths):
    offsets = jnp.arange(-RAD, RAD + 1).astype(jnp.float32)
    raw = jnp.exp(-offsets[None, :] ** 2 / (2.0 * kernel_widths[:, None] ** 2))
    return raw / jnp.sum(raw, axis=1, keepdims=True)


def tap_table(taps, distance):
    table = jnp.zeros((taps.shape[0],) + distance.shape, jnp.float32)
    for step in range(2 * RAD + 1):
        table = table + taps[:, step][:, None, None] * (distance == step).astype(jnp.float32)[None]
    return table


def smooth_all(padded, taps, planes, rows):
    columns = padded.shape[2]
    source = jnp.arange(columns, dtype=jnp.int32)
    circular = (source[:, None] - source[None, :] + RAD) % columns
    across_table = tap_table(taps, circular)
    across = jnp.einsum("prs,kst->kprt", padded, across_table, precision=exact_mode)
    row_out = jnp.arange(rows, dtype=jnp.int32)
    row_in = jnp.arange(rows + 2 * RAD, dtype=jnp.int32)
    row_table = tap_table(taps, row_in[None, :] - row_out[:, None])
    lines = jnp.einsum("kqr,kprt->kpqt", row_table, across, precision=exact_mode)
    plane_out = jnp.arange(planes, dtype=jnp.int32)
    plane_in = jnp.arange(planes + 2 * RAD, dtype=jnp.int32)
    plane_table = tap_table(taps, plane_in[None, :] - plane_out[:, None])
    return jnp.einsum("kop,kpqt->koqt", plane_table, lines, precision=exact_mode)


def network(features, w_in, b_in, w_mid, b_mid, w_out, b_out):
    count = features.shape[1]
    blocks = features.reshape(CHAN, count // CELL_BLOCK, CELL_BLOCK).transpose(1, 0, 2)

    def layer_stack(block):
        hidden = jax.nn.silu(jnp.dot(w_in.T, block, precision=exact_mode) + b_in[:, None])
        hidden = jax.nn.silu(jnp.dot(w_mid.T, hidden, precision=exact_mode) + b_mid[:, None])
        return jnp.dot(w_out, hidden, precision=exact_mode) + b_out[0]

    return lax.map(layer_stack, blocks).reshape(count)


def local(orbitals, occupation, corners, kernel_widths, w_in, b_in, w_mid, b_mid, w_out, b_out):
    slab_count = lax.axis_size("gz")
    slot_count = slab_count * CAP
    held = orbitals.shape[0]
    orbital_vals = orbitals.astype(jnp.float32)
    box_density = (occupation[:, None, None] * orbital_vals * orbital_vals).astype(jnp.bfloat16)
    box_density = box_density.reshape(held, BOX**3)
    target = corners[:, 0] // CZ
    orbital_ids = jnp.arange(held, dtype=jnp.int32)
    earlier = (target[:, None] == target[None, :]) & (orbital_ids[None, :] < orbital_ids[:, None])
    slot_rank = jnp.sum(earlier.astype(jnp.int32), axis=1)
    slot_of = target * CAP + slot_rank
    placer = (jnp.arange(slot_count, dtype=jnp.int32)[:, None] == slot_of[None, :]).astype(
        jnp.bfloat16
    )
    local_offsets = jnp.stack(
        [corners[:, 0] % CZ, corners[:, 1] % CY, corners[:, 2]], axis=1
    ).astype(jnp.bfloat16)
    sent = jnp.dot(placer, box_density, preferred_element_type=jnp.float32).astype(jnp.bfloat16)
    sent_offsets = jnp.dot(placer, local_offsets, preferred_element_type=jnp.float32).astype(
        jnp.bfloat16
    )
    received, received_offsets = (
        lax.all_to_all(
            sent.reshape(slab_count, CAP, BOX**3), "gz", split_axis=0, concat_axis=0, tiled=True
        ),
        lax.all_to_all(
            sent_offsets.reshape(slab_count, CAP, 3), "gz", split_axis=0, concat_axis=0, tiled=True
        ),
    )
    offsets = received_offsets.astype(jnp.float32).astype(jnp.int32)

    def deposit(source, grid):
        for column in range(CAP):
            piece = received[source, column].astype(jnp.float32).reshape(BOX, BOX, BOX)
            start = (
                offsets[source, column, 0],
                offsets[source, column, 1],
                offsets[source, column, 2],
            )
            region = lax.dynamic_slice(grid, start, (BOX, BOX, BOX))
            grid = lax.dynamic_update_slice(grid, region + piece, start)
        return grid

    extended = lax.fori_loop(
        0, slab_count, deposit, jnp.zeros((CZ + BOX, CY + BOX, NX + BOX), jnp.float32)
    )
    extended = extended[:, :, :NX].at[:, :, :BOX].add(extended[:, :, NX:])
    from_below = shifted(extended[CZ:].astype(jnp.bfloat16), "gz", 1).astype(jnp.float32)
    core = extended[:CZ].at[:BOX].add(from_below)
    from_left = shifted(core[:, CY:].astype(jnp.bfloat16), "gy", 1).astype(jnp.float32)
    tile = core[:, :CY].at[:, :BOX].add(from_left)
    density = lax.psum(tile.astype(jnp.bfloat16), "orb").astype(jnp.float32)
    padded = extended_2(density.astype(jnp.bfloat16), (("gz", 0), ("gy", 1)), RAD).astype(
        density.dtype
    )
    taps = kernel_taps(kernel_widths)
    features = jnp.log1p(smooth_all(padded, taps, CZ, CY))
    values = network(features.reshape(CHAN, CZ * CY * NX), w_in, b_in, w_mid, b_mid, w_out, b_out)
    potential = values.reshape(CZ, CY, NX).astype(jnp.bfloat16)
    next_rows = shifted(potential, "gy", -1)
    wide = jnp.concatenate([potential, next_rows], axis=1)
    next_planes = shifted(wide, "gz", -1)
    reach = jnp.concatenate([wide, next_planes], axis=0)
    reach = jnp.concatenate([reach, reach[:, :, :BOX]], axis=2)

    def cut(offset_row):
        windows = []
        for column in range(CAP):
            start = (offset_row[column, 0], offset_row[column, 1], offset_row[column, 2])
            window = lax.dynamic_slice(reach, start, (BOX, BOX, BOX))
            windows.append(window.reshape(BOX**3))
        return jnp.stack(windows)

    windows = lax.map(cut, offsets)
    returned = jax.tree.map(
        lambda part, own: part.astype(own.dtype),
        lax.all_to_all(for_sending(windows), "gz", split_axis=0, concat_axis=0, tiled=True),
        windows,
    )
    on_boxes = jnp.dot(
        placer.T, returned.reshape(slot_count, BOX**3), preferred_element_type=jnp.float32
    )
    applied = (on_boxes.reshape(held, BOX, BOX * BOX) * orbital_vals).astype(jnp.bfloat16)
    return (potential, applied)


def solution(mesh):
    return jax.shard_map(
        local,
        mesh=mesh,
        in_specs=(
            P(("gz", "gy", "orb"), None, None),
            P(("gz", "gy", "orb")),
            P(("gz", "gy", "orb"), None),
            P(),
            P(),
            P(),
            P(),
            P(),
            P(),
            P(),
        ),
        out_specs=(P("gz", "gy", None), P(("gz", "gy", "orb"), None, None)),
        check_vma=False,
    )
```

profile of v0, /device:TPU:1, one launch (start us, length us, event | category | flops | bytes accessed | tf_op | source)
XLA Modules:
  0.0 1365.4 jit_solution(875957933590389903)
XLA Ops:
  10.4 10.0 all-to-all-start
  23.9 3.5 all-to-all-done
  27.3 4.7 all-to-all-start.1
  37.6 19.2 %all-to-all-done.1 = bf16[16,2,13824]{2,1,0:T(2,128)(2,1)} async-done(((bf16[16,2,13824]{2,1,0:T(2,128)(2,1)}), bf16[16,2,13824]{2,1,0:T(2,128)(2,1)}, u32[]{:S(2)}, u32[]{:S(2)}) %all-to-all-start.1) | async-done | bytes 884768 | tf_op jit(solution)/shard_map/all_to_all | solution.py:106
  57.1 825.2 %while.38 = (s32[]{:T(128)}, f32[48,48,152]{2,1,0:T(8,128)S(1)}, s32[16,2,3]{0,1,2:T(2,128)S(1)}, bf16[16,2,13824]{2,1,0:T(2,128)(2,1)}, s32[]{:T(128)}, /*index=5*/s32[]{:T(128)}, s32[]{:T(128)}, s32[]{:T(128)}) while((s32[]{:T(128)}, f32[48,48,152]{2,1,0:T(8,128)S(1)}, s32[16,2,3]{0,1,2:T(2,128)S(1)}, bf16[16,2,13824]{2,1,0:T(2,128)(2,1)}, ...), condition=%wide.region_3.4_spmd, body=%wide.region_2.3_spmd.sunk | while | flops 55316 | bytes 940409 | solution.py:127
  65.0 16.9 %dynamic_update_slice.27 = f32[48,48,152]{2,1,0:T(8,128)S(1)} dynamic-update-slice(f32[48,48,152]{2,1,0:T(8,128)S(1)} %get-tuple-element.505, f32[24,24,24]{2,1,0:T(8,128)S(1)} %dynamic-slice_add_fusion.4, s32[]{:T(128)S(6)} %select_n.230, s32[]{:T(128)S(6)} %select_n.231, s32[]{:T(128)S(6)} %select_n.232) | dynamic-update-slice | bytes 110596 | tf_op jit(solution)/shard_map/while/body/eval_jaxpr/dynamic_update_slice | solution.py:124
  88.4 16.8 %dynamic_update_slice.28 = f32[48,48,152]{2,1,0:T(8,128)S(1)} dynamic-update-slice(f32[48,48,152]{2,1,0:T(8,128)S(1)} %dynamic_update_slice.27, f32[24,24,24]{2,1,0:T(8,128)S(1)} %dynamic-slice_add_fusion.5, s32[]{:T(128)S(6)} %select_n.233, s32[]{:T(128)S(6)} %select_n.234, s32[]{:T(128)S(6)} %select_n.235) | dynamic-update-slice | bytes 110596 | tf_op jit(solution)/shard_map/while/body/eval_jaxpr/dynamic_update_slice | solution.py:124
  113.0 23.0 %dynamic_update_slice.27 = f32[48,48,152]{2,1,0:T(8,128)S(1)} dynamic-update-slice(f32[48,48,152]{2,1,0:T(8,128)S(1)} %get-tuple-element.505, f32[24,24,24]{2,1,0:T(8,128)S(1)} %dynamic-slice_add_fusion.4, s32[]{:T(128)S(6)} %select_n.230, s32[]{:T(128)S(6)} %select_n.231, s32[]{:T(128)S(6)} %select_n.232) | dynamic-update-slice | bytes 110596 | tf_op jit(solution)/shard_map/while/body/eval_jaxpr/dynamic_update_slice | solution.py:124
  142.6 20.9 %dynamic_update_slice.28 = f32[48,48,152]{2,1,0:T(8,128)S(1)} dynamic-update-slice(f32[48,48,152]{2,1,0:T(8,128)S(1)} %dynamic_update_slice.27, f32[24,24,24]{2,1,0:T(8,128)S(1)} %dynamic-slice_add_fusion.5, s32[]{:T(128)S(6)} %select_n.233, s32[]{:T(128)S(6)} %select_n.234, s32[]{:T(128)S(6)} %select_n.235) | dynamic-update-slice | bytes 110596 | tf_op jit(solution)/shard_map/while/body/eval_jaxpr/dynamic_update_slice | solution.py:124
  171.3 22.8 %dynamic_update_slice.27 = f32[48,48,152]{2,1,0:T(8,128)S(1)} dynamic-update-slice(f32[48,48,152]{2,1,0:T(8,128)S(1)} %get-tuple-element.505, f32[24,24,24]{2,1,0:T(8,128)S(1)} %dynamic-slice_add_fusion.4, s32[]{:T(128)S(6)} %select_n.230, s32[]{:T(128)S(6)} %select_n.231, s32[]{:T(128)S(6)} %select_n.232) | dynamic-update-slice | bytes 110596 | tf_op jit(solution)/shard_map/while/body/eval_jaxpr/dynamic_update_slice | solution.py:124
  200.7 16.8 %dynamic_update_slice.28 = f32[48,48,152]{2,1,0:T(8,128)S(1)} dynamic-update-slice(f32[48,48,152]{2,1,0:T(8,128)S(1)} %dynamic_update_slice.27, f32[24,24,24]{2,1,0:T(8,128)S(1)} %dynamic-slice_add_fusion.5, s32[]{:T(128)S(6)} %select_n.233, s32[]{:T(128)S(6)} %select_n.234, s32[]{:T(128)S(6)} %select_n.235) | dynamic-update-slice | bytes 110596 | tf_op jit(solution)/shard_map/while/body/eval_jaxpr/dynamic_update_slice | solution.py:124
  225.3 20.7 %dynamic_update_slice.27 = f32[48,48,152]{2,1,0:T(8,128)S(1)} dynamic-update-slice(f32[48,48,152]{2,1,0:T(8,128)S(1)} %get-tuple-element.505, f32[24,24,24]{2,1,0:T(8,128)S(1)} %dynamic-slice_add_fusion.4, s32[]{:T(128)S(6)} %select_n.230, s32[]{:T(128)S(6)} %select_n.231, s32[]{:T(128)S(6)} %select_n.232) | dynamic-update-slice | bytes 110596 | tf_op jit(solution)/shard_map/while/body/eval_jaxpr/dynamic_update_slice | solution.py:124
  252.6 16.8 %dynamic_update_slice.28 = f32[48,48,152]{2,1,0:T(8,128)S(1)} dynamic-update-slice(f32[48,48,152]{2,1,0:T(8,128)S(1)} %dynamic_update_slice.27, f32[24,24,24]{2,1,0:T(8,128)S(1)} %dynamic-slice_add_fusion.5, s32[]{:T(128)S(6)} %select_n.233, s32[]{:T(128)S(6)} %select_n.234, s32[]{:T(128)S(6)} %select_n.235) | dynamic-update-slice | bytes 110596 | tf_op jit(solution)/shard_map/while/body/eval_jaxpr/dynamic_update_slice | solution.py:124
  277.2 19.7 %dynamic_update_slice.27 = f32[48,48,152]{2,1,0:T(8,128)S(1)} dynamic-update-slice(f32[48,48,152]{2,1,0:T(8,128)S(1)} %get-tuple-element.505, f32[24,24,24]{2,1,0:T(8,128)S(1)} %dynamic-slice_add_fusion.4, s32[]{:T(128)S(6)} %select_n.230, s32[]{:T(128)S(6)} %select_n.231, s32[]{:T(128)S(6)} %select_n.232) | dynamic-update-slice | bytes 110596 | tf_op jit(solution)/shard_map/while/body/eval_jaxpr/dynamic_update_slice | solution.py:124
  303.5 16.8 %dynamic_update_slice.28 = f32[48,48,152]{2,1,0:T(8,128)S(1)} dynamic-update-slice(f32[48,48,152]{2,1,0:T(8,128)S(1)} %dynamic_update_slice.27, f32[24,24,24]{2,1,0:T(8,128)S(1)} %dynamic-slice_add_fusion.5, s32[]{:T(128)S(6)} %select_n.233, s32[]{:T(128)S(6)} %select_n.234, s32[]{:T(128)S(6)} %select_n.235) | dynamic-update-slice | bytes 110596 | tf_op jit(solution)/shard_map/while/body/eval_jaxpr/dynamic_update_slice | solution.py:124
  328.2 16.8 %dynamic_update_slice.27 = f32[48,48,152]{2,1,0:T(8,128)S(1)} dynamic-update-slice(f32[48,48,152]{2,1,0:T(8,128)S(1)} %get-tuple-element.505, f32[24,24,24]{2,1,0:T(8,128)S(1)} %dynamic-slice_add_fusion.4, s32[]{:T(128)S(6)} %select_n.230, s32[]{:T(128)S(6)} %select_n.231, s32[]{:T(128)S(6)} %select_n.232) | dynamic-update-slice | bytes 110596 | tf_op jit(solution)/shard_map/while/body/eval_jaxpr/dynamic_update_slice | solution.py:124
  351.5 16.8 %dynamic_update_slice.28 = f32[48,48,152]{2,1,0:T(8,128)S(1)} dynamic-update-slice(f32[48,48,152]{2,1,0:T(8,128)S(1)} %dynamic_update_slice.27, f32[24,24,24]{2,1,0:T(8,128)S(1)} %dynamic-slice_add_fusion.5, s32[]{:T(128)S(6)} %select_n.233, s32[]{:T(128)S(6)} %select_n.234, s32[]{:T(128)S(6)} %select_n.235) | dynamic-update-slice | bytes 110596 | tf_op jit(solution)/shard_map/while/body/eval_jaxpr/dynamic_update_slice | solution.py:124
  376.2 22.1 %dynamic_update_slice.27 = f32[48,48,152]{2,1,0:T(8,128)S(1)} dynamic-update-slice(f32[48,48,152]{2,1,0:T(8,128)S(1)} %get-tuple-element.505, f32[24,24,24]{2,1,0:T(8,128)S(1)} %dynamic-slice_add_fusion.4, s32[]{:T(128)S(6)} %select_n.230, s32[]{:T(128)S(6)} %select_n.231, s32[]{:T(128)S(6)} %select_n.232) | dynamic-update-slice | bytes 110596 | tf_op jit(solution)/shard_map/while/body/eval_jaxpr/dynamic_update_slice | solution.py:124
  404.8 16.8 %dynamic_update_slice.28 = f32[48,48,152]{2,1,0:T(8,128)S(1)} dynamic-update-slice(f32[48,48,152]{2,1,0:T(8,128)S(1)} %dynamic_update_slice.27, f32[24,24,24]{2,1,0:T(8,128)S(1)} %dynamic-slice_add_fusion.5, s32[]{:T(128)S(6)} %select_n.233, s32[]{:T(128)S(6)} %select_n.234, s32[]{:T(128)S(6)} %select_n.235) | dynamic-update-slice | bytes 110596 | tf_op jit(solution)/shard_map/while/body/eval_jaxpr/dynamic_update_slice | solution.py:124
  429.4 21.6 %dynamic_update_slice.27 = f32[48,48,152]{2,1,0:T(8,128)S(1)} dynamic-update-slice(f32[48,48,152]{2,1,0:T(8,128)S(1)} %get-tuple-element.505, f32[24,24,24]{2,1,0:T(8,128)S(1)} %dynamic-slice_add_fusion.4, s32[]{:T(128)S(6)} %select_n.230, s32[]{:T(128)S(6)} %select_n.231, s32[]{:T(128)S(6)} %select_n.232) | dynamic-update-slice | bytes 110596 | tf_op jit(solution)/shard_map/while/body/eval_jaxpr/dynamic_update_slice | solution.py:124
  457.6 19.7 %dynamic_update_slice.28 = f32[48,48,152]{2,1,0:T(8,128)S(1)} dynamic-update-slice(f32[48,48,152]{2,1,0:T(8,128)S(1)} %dynamic_update_slice.27, f32[24,24,24]{2,1,0:T(8,128)S(1)} %dynamic-slice_add_fusion.5, s32[]{:T(128)S(6)} %select_n.233, s32[]{:T(128)S(6)} %select_n.234, s32[]{:T(128)S(6)} %select_n.235) | dynamic-update-slice | bytes 110596 | tf_op jit(solution)/shard_map/while/body/eval_jaxpr/dynamic_update_slice | solution.py:124
  485.2 17.9 %dynamic_update_slice.27 = f32[48,48,152]{2,1,0:T(8,128)S(1)} dynamic-update-slice(f32[48,48,152]{2,1,0:T(8,128)S(1)} %get-tuple-element.505, f32[24,24,24]{2,1,0:T(8,128)S(1)} %dynamic-slice_add_fusion.4, s32[]{:T(128)S(6)} %select_n.230, s32[]{:T(128)S(6)} %select_n.231, s32[]{:T(128)S(6)} %select_n.232) | dynamic-update-slice | bytes 110596 | tf_op jit(solution)/shard_map/while/body/eval_jaxpr/dynamic_update_slice | solution.py:124
  509.6 19.5 %dynamic_update_slice.28 = f32[48,48,152]{2,1,0:T(8,128)S(1)} dynamic-update-slice(f32[48,48,152]{2,1,0:T(8,128)S(1)} %dynamic_update_slice.27, f32[24,24,24]{2,1,0:T(8,128)S(1)} %dynamic-slice_add_fusion.5, s32[]{:T(128)S(6)} %select_n.233, s32[]{:T(128)S(6)} %select_n.234, s32[]{:T(128)S(6)} %select_n.235) | dynamic-update-slice | bytes 110596 | tf_op jit(solution)/shard_map/while/body/eval_jaxpr/dynamic_update_slice | solution.py:124
  537.0 18.6 %dynamic_update_slice.27 = f32[48,48,152]{2,1,0:T(8,128)S(1)} dynamic-update-slice(f32[48,48,152]{2,1,0:T(8,128)S(1)} %get-tuple-element.505, f32[24,24,24]{2,1,0:T(8,128)S(1)} %dynamic-slice_add_fusion.4, s32[]{:T(128)S(6)} %select_n.230, s32[]{:T(128)S(6)} %select_n.231, s32[]{:T(128)S(6)} %select_n.232) | dynamic-update-slice | bytes 110596 | tf_op jit(solution)/shard_map/while/body/eval_jaxpr/dynamic_update_slice | solution.py:124
  562.1 16.8 %dynamic_update_slice.28 = f32[48,48,152]{2,1,0:T(8,128)S(1)} dynamic-update-slice(f32[48,48,152]{2,1,0:T(8,128)S(1)} %dynamic_update_slice.27, f32[24,24,24]{2,1,0:T(8,128)S(1)} %dynamic-slice_add_fusion.5, s32[]{:T(128)S(6)} %select_n.233, s32[]{:T(128)S(6)} %select_n.234, s32[]{:T(128)S(6)} %select_n.235) | dynamic-update-slice | bytes 110596 | tf_op jit(solution)/shard_map/while/body/eval_jaxpr/dynamic_update_slice | solution.py:124
  586.8 19.4 %dynamic_update_slice.27 = f32[48,48,152]{2,1,0:T(8,128)S(1)} dynamic-update-slice(f32[48,48,152]{2,1,0:T(8,128)S(1)} %get-tuple-element.505, f32[24,24,24]{2,1,0:T(8,128)S(1)} %dynamic-slice_add_fusion.4, s32[]{:T(128)S(6)} %select_n.230, s32[]{:T(128)S(6)} %select_n.231, s32[]{:T(128)S(6)} %select_n.232) | dynamic-update-slice | bytes 110596 | tf_op jit(solution)/shard_map/while/body/eval_jaxpr/dynamic_update_slice | solution.py:124
  612.8 16.8 %dynamic_update_slice.28 = f32[48,48,152]{2,1,0:T(8,128)S(1)} dynamic-update-slice(f32[48,48,152]{2,1,0:T(8,128)S(1)} %dynamic_update_slice.27, f32[24,24,24]{2,1,0:T(8,128)S(1)} %dynamic-slice_add_fusion.5, s32[]{:T(128)S(6)} %select_n.233, s32[]{:T(128)S(6)} %select_n.234, s32[]{:T(128)S(6)} %select_n.235) | dynamic-update-slice | bytes 110596 | tf_op jit(solution)/shard_map/while/body/eval_jaxpr/dynamic_update_slice | solution.py:124
  637.4 18.9 %dynamic_update_slice.27 = f32[48,48,152]{2,1,0:T(8,128)S(1)} dynamic-update-slice(f32[48,48,152]{2,1,0:T(8,128)S(1)} %get-tuple-element.505, f32[24,24,24]{2,1,0:T(8,128)S(1)} %dynamic-slice_add_fusion.4, s32[]{:T(128)S(6)} %select_n.230, s32[]{:T(128)S(6)} %select_n.231, s32[]{:T(128)S(6)} %select_n.232) | dynamic-update-slice | bytes 110596 | tf_op jit(solution)/shard_map/while/body/eval_jaxpr/dynamic_update_slice | solution.py:124
  662.9 16.8 %dynamic_update_slice.28 = f32[48,48,152]{2,1,0:T(8,128)S(1)} dynamic-update-slice(f32[48,48,152]{2,1,0:T(8,128)S(1)} %dynamic_update_slice.27, f32[24,24,24]{2,1,0:T(8,128)S(1)} %dynamic-slice_add_fusion.5, s32[]{:T(128)S(6)} %select_n.233, s32[]{:T(128)S(6)} %select_n.234, s32[]{:T(128)S(6)} %select_n.235) | dynamic-update-slice | bytes 110596 | tf_op jit(solution)/shard_map/while/body/eval_jaxpr/dynamic_update_slice | solution.py:124
  687.6 11.6 dynamic_update_slice.27
  705.8 16.8 %dynamic_update_slice.28 = f32[48,48,152]{2,1,0:T(8,128)S(1)} dynamic-update-slice(f32[48,48,152]{2,1,0:T(8,128)S(1)} %dynamic_update_slice.27, f32[24,24,24]{2,1,0:T(8,128)S(1)} %dynamic-slice_add_fusion.5, s32[]{:T(128)S(6)} %select_n.233, s32[]{:T(128)S(6)} %select_n.234, s32[]{:T(128)S(6)} %select_n.235) | dynamic-update-slice | bytes 110596 | tf_op jit(solution)/shard_map/while/body/eval_jaxpr/dynamic_update_slice | solution.py:124
  730.4 19.7 %dynamic_update_slice.27 = f32[48,48,152]{2,1,0:T(8,128)S(1)} dynamic-update-slice(f32[48,48,152]{2,1,0:T(8,128)S(1)} %get-tuple-element.505, f32[24,24,24]{2,1,0:T(8,128)S(1)} %dynamic-slice_add_fusion.4, s32[]{:T(128)S(6)} %select_n.230, s32[]{:T(128)S(6)} %select_n.231, s32[]{:T(128)S(6)} %select_n.232) | dynamic-update-slice | bytes 110596 | tf_op jit(solution)/shard_map/while/body/eval_jaxpr/dynamic_update_slice | solution.py:124
  756.7 19.7 %dynamic_update_slice.28 = f32[48,48,152]{2,1,0:T(8,128)S(1)} dynamic-update-slice(f32[48,48,152]{2,1,0:T(8,128)S(1)} %dynamic_update_slice.27, f32[24,24,24]{2,1,0:T(8,128)S(1)} %dynamic-slice_add_fusion.5, s32[]{:T(128)S(6)} %select_n.233, s32[]{:T(128)S(6)} %select_n.234, s32[]{:T(128)S(6)} %select_n.235) | dynamic-update-slice | bytes 110596 | tf_op jit(solution)/shard_map/while/body/eval_jaxpr/dynamic_update_slice | solution.py:124
  784.3 20.5 %dynamic_update_slice.27 = f32[48,48,152]{2,1,0:T(8,128)S(1)} dynamic-update-slice(f32[48,48,152]{2,1,0:T(8,128)S(1)} %get-tuple-element.505, f32[24,24,24]{2,1,0:T(8,128)S(1)} %dynamic-slice_add_fusion.4, s32[]{:T(128)S(6)} %select_n.230, s32[]{:T(128)S(6)} %select_n.231, s32[]{:T(128)S(6)} %select_n.232) | dynamic-update-slice | bytes 110596 | tf_op jit(solution)/shard_map/while/body/eval_jaxpr/dynamic_update_slice | solution.py:124
  811.3 18.5 %dynamic_update_slice.28 = f32[48,48,152]{2,1,0:T(8,128)S(1)} dynamic-update-slice(f32[48,48,152]{2,1,0:T(8,128)S(1)} %dynamic_update_slice.27, f32[24,24,24]{2,1,0:T(8,128)S(1)} %dynamic-slice_add_fusion.5, s32[]{:T(128)S(6)} %select_n.233, s32[]{:T(128)S(6)} %select_n.234, s32[]{:T(128)S(6)} %select_n.235) | dynamic-update-slice | bytes 110596 | tf_op jit(solution)/shard_map/while/body/eval_jaxpr/dynamic_update_slice | solution.py:124
  837.7 18.1 %dynamic_update_slice.27 = f32[48,48,152]{2,1,0:T(8,128)S(1)} dynamic-update-slice(f32[48,48,152]{2,1,0:T(8,128)S(1)} %get-tuple-element.505, f32[24,24,24]{2,1,0:T(8,128)S(1)} %dynamic-slice_add_fusion.4, s32[]{:T(128)S(6)} %select_n.230, s32[]{:T(128)S(6)} %select_n.231, s32[]{:T(128)S(6)} %select_n.232) | dynamic-update-slice | bytes 110596 | tf_op jit(solution)/shard_map/while/body/eval_jaxpr/dynamic_update_slice | solution.py:124
  862.4 19.9 %dynamic_update_slice.28 = f32[48,48,152]{2,1,0:T(8,128)S(1)} dynamic-update-slice(f32[48,48,152]{2,1,0:T(8,128)S(1)} %dynamic_update_slice.27, f32[24,24,24]{2,1,0:T(8,128)S(1)} %dynamic-slice_add_fusion.5, s32[]{:T(128)S(6)} %select_n.233, s32[]{:T(128)S(6)} %select_n.234, s32[]{:T(128)S(6)} %select_n.235) | dynamic-update-slice | bytes 110596 | tf_op jit(solution)/shard_map/while/body/eval_jaxpr/dynamic_update_slice | solution.py:124
  883.6 6.9 scatter-add.4
  892.7 2.6 collective-permute-done
  896.5 4.0 collective-permute-start.1
  900.6 3.6 collective-permute-done.1
  905.0 87.0 %all-reduce.2.cloned.1.call-done = bf16[24,24,128]{2,1,0:T(8,128)(2,1)} async-done(((bf16[24,24,128]{2,1,0:T(8,128)(2,1)}), bf16[24,24,128]{2,1,0:T(8,128)(2,1)}) %all-reduce.2.cloned.1.call-update) | async-done | bytes 147472 | tf_op jit(solution)/shard_map/psum | solution.py:135
  1001.0 2.7 collective-permute-start.5
  1006.9 3.1 fusion.33
  1010.0 4.9 fusion.23
  1014.9 3.4 fusion.26
  1021.0 77.4 %while.39 = (s32[]{:T(128)}, bf16[6,12288]{1,0:T(8,128)(2,1)S(1)}, f32[6,8,12288]{2,0,1:T(8,128)}, f32[8,64]{1,0:T(8,128)S(1)}, f32[64]{0:T(128)S(1)}, /*index=5...) while((s32[]{:T(128)}, bf16[6,12288]{1,0:T(8,128)(2,1)S(1)}, ...), condition=%wide.region_6.7_spmd, body=%wide.region_5.6_spmd.sunk | while | flops 696791040 | bytes 14027641 | solution.py:80
  1023.3 2.7 fusion.161
  1026.0 3.8 fusion.162
  1036.2 2.7 fusion.161
  1038.9 3.8 fusion.162
  1049.1 2.7 fusion.161
  1051.8 3.8 fusion.162
  1062.0 2.7 fusion.161
  1064.7 3.8 fusion.162
  1074.9 2.7 fusion.161
  1077.6 3.8 fusion.162
  1087.8 2.7 fusion.161
  1090.5 3.8 fusion.162
  1098.7 3.8 collective-permute-start.6
  1104.6 3.3 collective-permute-start.7
  1107.9 4.9 collective-permute-done.7
  1112.8 211.0 %while.40 = (s32[]{:T(128)}, bf16[16,2,13824]{2,1,0:T(2,128)(2,1)S(1)}, s32[16,2,3]{2,1,0:T(2,128)}, bf16[48,48,152]{2,1,0:T(8,128)(2,1)S(1)}, s32[]{:T(128)}, /*index=5*/s32[]{:T(128)}, s32[]{:T(128)}, s32[]{:T(128)}) while((s32[]{:T(128)}, bf16[16,2,13824]{2,1,0:T(2,128)(2,1)S(1)}, s32[16,2,3]{2,1,0:T(2,128)}, ...), condition=%wide.region_8.9_spmd, body=%wide.region_7.8_spmd.sunk | while | flops 110612 | bytes 387489 | solution.py:157
  1323.9 32.4 %all_to_all.15 = bf16[16,2,13824]{2,1,0:T(2,128)(2,1)S(1)} all-to-all(bf16[16,2,13824]{2,1,0:T(2,128)(2,1)S(1)} %get-tuple-element.204), channel_id=1, replica_groups=mesh['gz'=16,'gy'=8,'orb'=2] {'gz'}, dimensions={0} | all-to-all | bytes 1769472 | tf_op jit(solution)/shard_map/all_to_all | solution.py:160
  (327 shorter events, 152.8 us)
Async XLA Ops:
  10.4 16.9 %all-to-all-start = ((bf16[16,2,3]{2,1,0:T(2,128)(2,1)}), bf16[16,2,3]{2,1,0:T(2,128)(2,1)S(1)}, u32[]{:S(2)}, u32[]{:S(2)}) async-start(bf16[16,2,3]{2,1,0:T(2,128)(2,1)} %bitcast.41), calls=%async_computation | async-start | bytes 16384 | tf_op jit(solution)/shard_map/all_to_all | solution.py:109
  21.8 11.6 copy-start.18
  27.3 29.5 %all-to-all-start.1 = ((bf16[16,2,13824]{2,1,0:T(2,128)(2,1)}), bf16[16,2,13824]{2,1,0:T(2,128)(2,1)}, u32[]{:S(2)}, u32[]{:S(2)}) async-start(bf16[16,2,13824]{2,1,0:T(2,128)(2,1)} %reshape.511), calls=%async_computation.1 | async-start | bytes 1769472 | tf_op jit(solution)/shard_map/all_to_all | solution.py:106
  32.0 960.0 %all-reduce.2.cloned.1.call-start = ((), (), s32[]{:S(2)}) async-start(), calls=%async_computation.3 | async-start | bytes 294912 | tf_op jit(solution)/shard_map/psum | solution.py:135
  37.5 19.6 %copy-start.15 = (s32[16,2,3]{2,1,0:T(2,128)}, s32[16,2,3]{2,1,0:T(2,128)S(1)}, u32[]{:S(2)}) copy-start(s32[16,2,3]{2,1,0:T(2,128)S(1)} %convert_convert_fusion) | copy-start | bytes 1156
  883.5 123.3 %copy-start.2 = (f32[128,128]{1,0:T(8,128)S(1)}, f32[128,128]{1,0:T(8,128)}, u32[]{:S(2)}) copy-start(f32[128,128]{1,0:T(8,128)} %compare_convert_fusion.12) | copy-start | bytes 196612
  883.5 123.2 %copy-start.3 = (f32[128,128]{1,0:T(8,128)S(1)}, f32[128,128]{1,0:T(8,128)}, u32[]{:S(2)}) copy-start(f32[128,128]{1,0:T(8,128)} %get-tuple-element.335) | copy-start | bytes 196612
  883.6 123.2 %copy-start.4 = (f32[128,128]{1,0:T(8,128)S(1)}, f32[128,128]{1,0:T(8,128)}, u32[]{:S(2)}) copy-start(f32[128,128]{1,0:T(8,128)} %get-tuple-element.336) | copy-start | bytes 196612
  883.6 123.2 %copy-start.5 = (f32[128,128]{1,0:T(8,128)S(1)}, f32[128,128]{1,0:T(8,128)}, u32[]{:S(2)}) copy-start(f32[128,128]{1,0:T(8,128)} %get-tuple-element.337) | copy-start | bytes 196612
  883.6 123.2 %copy-start.6 = (f32[128,128]{1,0:T(8,128)S(1)}, f32[128,128]{1,0:T(8,128)}, u32[]{:S(2)}) copy-start(f32[128,128]{1,0:T(8,128)} %get-tuple-element.338) | copy-start | bytes 196612
  883.6 123.2 %copy-start.7 = (f32[128,128]{1,0:T(8,128)S(1)}, f32[128,128]{1,0:T(8,128)}, u32[]{:S(2)}) copy-start(f32[128,128]{1,0:T(8,128)} %get-tuple-element.339) | copy-start | bytes 196612
  883.6 123.2 %copy-start.8 = (f32[128,128]{1,0:T(8,128)S(1)}, f32[128,128]{1,0:T(8,128)}, u32[]{:S(2)}) copy-start(f32[128,128]{1,0:T(8,128)} %get-tuple-element.340) | copy-start | bytes 196612
  883.6 123.2 %copy-start.9 = (f32[128,128]{1,0:T(8,128)S(1)}, f32[128,128]{1,0:T(8,128)}, u32[]{:S(2)}) copy-start(f32[128,128]{1,0:T(8,128)} %get-tuple-element.341) | copy-start | bytes 196612
  883.6 123.2 %copy-start.10 = (f32[128,128]{1,0:T(8,128)S(1)}, f32[128,128]{1,0:T(8,128)}, u32[]{:S(2)}) copy-start(f32[128,128]{1,0:T(8,128)} %get-tuple-element.342) | copy-start | bytes 196612
  891.7 3.7 collective-permute-start
  896.5 7.7 collective-permute-start.1
  992.8 3.3 collective-permute-start.2
  995.1 3.4 collective-permute-start.3
  998.5 6.9 collective-permute-start.4
  1001.0 5.8 collective-permute-start.5
  1006.8 3.2 copy-start.11
  1006.9 3.2 copy-start.12
  1006.9 3.2 copy-start.13
  1018.8 2.2 copy-start.14
  1018.8 2.2 copy-start.16
  1018.8 2.2 copy-start.17
  1018.8 2.2 copy-start.19
  1018.8 2.2 copy-start.20
  1098.6 14.2 %copy-start.1 = (bf16[24,24,128]{2,1,0:T(8,128)(2,1)}, bf16[24,24,128]{2,1,0:T(8,128)(2,1)S(1)}, u32[]{:S(2)}) copy-start(bf16[24,24,128]{2,1,0:T(8,128)(2,1)S(1)} %convert_element_type.308) | copy-start | bytes 442372
  1098.7 5.9 collective-permute-start.6
  1104.6 8.2 collective-permute-start.7
  1323.8 33.5 %copy-start = (bf16[16,24,576]{2,1,0:T(8,128)(2,1)S(1)}, bf16[16,24,576]{2,1,0:T(8,128)(2,1)}, u32[]{:S(2)}) copy-start(bf16[16,24,576]{2,1,0:T(8,128)(2,1)} %param.26) | copy-start | bytes 1327108
Sparse Core Ops, SparseCore 0:
  905.0 86.9 all-reduce.1
where the time goes:
time: 1370 us
  local copies, waits for them, and re-layouts  685 us (50%)
  loops' own time  365 us (27%)
  waiting for transfers between devices  128 us (9%)
  matrix products  65.3 us (5%)
  other arithmetic  42 us (3%)
  starting transfers between devices  33.3 us (2%)
  blocking collectives  32.4 us (2%)
  between operations  14.5 us (1%)
    dynamic_update_slice x32, local copies, waits for them, and re-layouts, deposit(): grid = lax.dynamic_update_slice(grid, region + piece, start)  595 us
    another operation x1, loops' own time, local(): lax.fori_loop(0, slab_count, deposit, jnp.zeros((CZ + BOX, CY + BOX, NX +...  189 us
    another operation x1, loops' own time, local(): windows = lax.map(cut, offsets)  176 us
    psum x1, waiting for transfers between devices, local(): density = lax.psum(tile.astype(jnp.bfloat16), 'orb').astype(jnp.float32)  87 us
    all_to_all x1, blocking collectives, local(): lax.all_to_all(for_sending(windows), 'gz', split_axis=0, concat_axis=0, t...  32.4 us
  transfers between devices with their start and end apart: 11, of which 11 were waited for; matrix products, arithmetic and copies ran while one was open for 1% of the time, Pallas kernels for 0%

commit v1 on v0

--- a/solution.py
+++ b/solution.py
@@ -132,7 +132,7 @@
     core = extended[:CZ].at[:BOX].add(from_below)
     from_left = shifted(core[:, CY:].astype(jnp.bfloat16), "gy", 1).astype(jnp.float32)
     tile = core[:, :CY].at[:, :BOX].add(from_left)
-    density = lax.psum(tile.astype(jnp.bfloat16), "orb").astype(jnp.float32)
+    density = jnp.sum(lax.all_gather(tile.astype(jnp.bfloat16), "orb"), axis=0).astype(jnp.float32)
     padded = extended_2(density.astype(jnp.bfloat16), (("gz", 0), ("gy", 1)), RAD).astype(
         density.dtype
     )

time: 1370 us -> 1320 us (0.964)
  waiting for transfers between devices: 128 us -> 33.3 us
  starting transfers between devices: 33.3 us -> 81.7 us
  blocking collectives: 32.4 us -> 47.1 us
    psum x1 -> x0, waiting for transfers between devices: 87 us -> none  [local(): density = lax.psum(tile.astype(jnp.bfloat16), 'orb').astype(jnp.float32)]
    ppermute x4, starting transfers between devices: 11.1 us -> 36.4 us  [shifted(): return lax.ppermute(x, axis, [(i, (i + by) % count) for i in range(count)])]
    ppermute x2, starting transfers between devices: 2.68 us -> 22.1 us  [extended_2(): lax.ppermute(head, axis, [((i + 1) % count, i) for i in range(count)])]
    all_gather x0 -> x1, blocking collectives: none -> 14.3 us  [local(): lax.all_gather(tile.astype(jnp.bfloat16), 'orb')]
  transfers between devices with their start and end apart: 11 -> 10, of which waited for: 11 -> 9; matrix products, arithmetic and copies ran while one was open for 1% -> 1% of each run, Pallas kernels for 0% -> 0%
where the time goes in v1:
time: 1320 us; the launch traced here: 1310 us
  local copies, waits for them, and re-layouts  683 us (52%)
  loops' own time  356 us (27%)
  starting transfers between devices  81.7 us (6%)
  matrix products  65.3 us (5%)
  blocking collectives  47.1 us (4%)
  other arithmetic  42.6 us (3%)
  waiting for transfers between devices  33.3 us (3%)
    dynamic_update_slice x32, local copies, waits for them, and re-layouts, deposit(): grid = lax.dynamic_update_slice(grid, region + piece, start)  595 us
    another operation x1, loops' own time, local(): lax.fori_loop(0, slab_count, deposit, jnp.zeros((CZ + BOX, CY + BOX, NX +...  180 us
    another operation x1, loops' own time, local(): windows = lax.map(cut, offsets)  176 us
    ppermute x4, starting transfers between devices, shifted(): return lax.ppermute(x, axis, [(i, (i + by) % count) for i in range(count)])  36.4 us
    all_to_all x1, blocking collectives, local(): lax.all_to_all(for_sending(windows), 'gz', split_axis=0, concat_axis=0, t...  32.9 us
  transfers between devices with their start and end apart: 10, of which 9 were waited for; matrix products, arithmetic and copies ran while one was open for 1% of the time, Pallas kernels for 0%

profile of v1, /device:TPU:1, one launch (start us, length us, event | category | flops | bytes accessed | tf_op | source)
XLA Modules:
  0.0 1310.4 jit_solution(10331546269419292402)
XLA Ops:
  3.9 10.0 all-to-all-start
  20.8 5.0 all-to-all-start.1
  31.4 19.1 %all-to-all-done.1 = bf16[16,2,13824]{2,1,0:T(2,128)(2,1)} async-done(((bf16[16,2,13824]{2,1,0:T(2,128)(2,1)}), bf16[16,2,13824]{2,1,0:T(2,128)(2,1)}, u32[]{:S(2)}, u32[]{:S(2)}) %all-to-all-start.1) | async-done | bytes 884768 | tf_op jit(solution)/shard_map/all_to_all | solution.py:106
  50.8 816.2 %while.38 = (s32[]{:T(128)}, f32[48,48,152]{2,1,0:T(8,128)S(1)}, s32[16,2,3]{0,1,2:T(2,128)S(1)}, bf16[16,2,13824]{2,1,0:T(2,128)(2,1)}, s32[]{:T(128)}, /*index=5*/s32[]{:T(128)}, s32[]{:T(128)}, s32[]{:T(128)}) while((s32[]{:T(128)}, f32[48,48,152]{2,1,0:T(8,128)S(1)}, s32[16,2,3]{0,1,2:T(2,128)S(1)}, bf16[16,2,13824]{2,1,0:T(2,128)(2,1)}, ...), condition=%wide.region_3.4_spmd, body=%wide.region_2.3_spmd.sunk | while | flops 55316 | bytes 940409 | solution.py:127
  58.5 16.9 %dynamic_update_slice.27 = f32[48,48,152]{2,1,0:T(8,128)S(1)} dynamic-update-slice(f32[48,48,152]{2,1,0:T(8,128)S(1)} %get-tuple-element.505, f32[24,24,24]{2,1,0:T(8,128)S(1)} %dynamic-slice_add_fusion.4, s32[]{:T(128)S(6)} %select_n.230, s32[]{:T(128)S(6)} %select_n.231, s32[]{:T(128)S(6)} %select_n.232) | dynamic-update-slice | bytes 110596 | tf_op jit(solution)/shard_map/while/body/eval_jaxpr/dynamic_update_slice | solution.py:124
  81.5 16.8 %dynamic_update_slice.28 = f32[48,48,152]{2,1,0:T(8,128)S(1)} dynamic-update-slice(f32[48,48,152]{2,1,0:T(8,128)S(1)} %dynamic_update_slice.27, f32[24,24,24]{2,1,0:T(8,128)S(1)} %dynamic-slice_add_fusion.5, s32[]{:T(128)S(6)} %select_n.233, s32[]{:T(128)S(6)} %select_n.234, s32[]{:T(128)S(6)} %select_n.235) | dynamic-update-slice | bytes 110596 | tf_op jit(solution)/shard_map/while/body/eval_jaxpr/dynamic_update_slice | solution.py:124
  106.0 23.0 %dynamic_update_slice.27 = f32[48,48,152]{2,1,0:T(8,128)S(1)} dynamic-update-slice(f32[48,48,152]{2,1,0:T(8,128)S(1)} %get-tuple-element.505, f32[24,24,24]{2,1,0:T(8,128)S(1)} %dynamic-slice_add_fusion.4, s32[]{:T(128)S(6)} %select_n.230, s32[]{:T(128)S(6)} %select_n.231, s32[]{:T(128)S(6)} %select_n.232) | dynamic-update-slice | bytes 110596 | tf_op jit(solution)/shard_map/while/body/eval_jaxpr/dynamic_update_slice | solution.py:124
  135.1 20.9 %dynamic_update_slice.28 = f32[48,48,152]{2,1,0:T(8,128)S(1)} dynamic-update-slice(f32[48,48,152]{2,1,0:T(8,128)S(1)} %dynamic_update_slice.27, f32[24,24,24]{2,1,0:T(8,128)S(1)} %dynamic-slice_add_fusion.5, s32[]{:T(128)S(6)} %select_n.233, s32[]{:T(128)S(6)} %select_n.234, s32[]{:T(128)S(6)} %select_n.235) | dynamic-update-slice | bytes 110596 | tf_op jit(solution)/shard_map/while/body/eval_jaxpr/dynamic_update_slice | solution.py:124
  163.8 22.8 %dynamic_update_slice.27 = f32[48,48,152]{2,1,0:T(8,128)S(1)} dynamic-update-slice(f32[48,48,152]{2,1,0:T(8,128)S(1)} %get-tuple-element.505, f32[24,24,24]{2,1,0:T(8,128)S(1)} %dynamic-slice_add_fusion.4, s32[]{:T(128)S(6)} %select_n.230, s32[]{:T(128)S(6)} %select_n.231, s32[]{:T(128)S(6)} %select_n.232) | dynamic-update-slice | bytes 110596 | tf_op jit(solution)/shard_map/while/body/eval_jaxpr/dynamic_update_slice | solution.py:124
  192.7 16.8 %dynamic_update_slice.28 = f32[48,48,152]{2,1,0:T(8,128)S(1)} dynamic-update-slice(f32[48,48,152]{2,1,0:T(8,128)S(1)} %dynamic_update_slice.27, f32[24,24,24]{2,1,0:T(8,128)S(1)} %dynamic-slice_add_fusion.5, s32[]{:T(128)S(6)} %select_n.233, s32[]{:T(128)S(6)} %select_n.234, s32[]{:T(128)S(6)} %select_n.235) | dynamic-update-slice | bytes 110596 | tf_op jit(solution)/shard_map/while/body/eval_jaxpr/dynamic_update_slice | solution.py:124
  217.2 20.7 %dynamic_update_slice.27 = f32[48,48,152]{2,1,0:T(8,128)S(1)} dynamic-update-slice(f32[48,48,152]{2,1,0:T(8,128)S(1)} %get-tuple-element.505, f32[24,24,24]{2,1,0:T(8,128)S(1)} %dynamic-slice_add_fusion.4, s32[]{:T(128)S(6)} %select_n.230, s32[]{:T(128)S(6)} %select_n.231, s32[]{:T(128)S(6)} %select_n.232) | dynamic-update-slice | bytes 110596 | tf_op jit(solution)/shard_map/while/body/eval_jaxpr/dynamic_update_slice | solution.py:124
  244.0 16.8 %dynamic_update_slice.28 = f32[48,48,152]{2,1,0:T(8,128)S(1)} dynamic-update-slice(f32[48,48,152]{2,1,0:T(8,128)S(1)} %dynamic_update_slice.27, f32[24,24,24]{2,1,0:T(8,128)S(1)} %dynamic-slice_add_fusion.5, s32[]{:T(128)S(6)} %select_n.233, s32[]{:T(128)S(6)} %select_n.234, s32[]{:T(128)S(6)} %select_n.235) | dynamic-update-slice | bytes 110596 | tf_op jit(solution)/shard_map/while/body/eval_jaxpr/dynamic_update_slice | solution.py:124
  268.6 19.7 %dynamic_update_slice.27 = f32[48,48,152]{2,1,0:T(8,128)S(1)} dynamic-update-slice(f32[48,48,152]{2,1,0:T(8,128)S(1)} %get-tuple-element.505, f32[24,24,24]{2,1,0:T(8,128)S(1)} %dynamic-slice_add_fusion.4, s32[]{:T(128)S(6)} %select_n.230, s32[]{:T(128)S(6)} %select_n.231, s32[]{:T(128)S(6)} %select_n.232) | dynamic-update-slice | bytes 110596 | tf_op jit(solution)/shard_map/while/body/eval_jaxpr/dynamic_update_slice | solution.py:124
  294.4 16.8 %dynamic_update_slice.28 = f32[48,48,152]{2,1,0:T(8,128)S(1)} dynamic-update-slice(f32[48,48,152]{2,1,0:T(8,128)S(1)} %dynamic_update_slice.27, f32[24,24,24]{2,1,0:T(8,128)S(1)} %dynamic-slice_add_fusion.5, s32[]{:T(128)S(6)} %select_n.233, s32[]{:T(128)S(6)} %select_n.234, s32[]{:T(128)S(6)} %select_n.235) | dynamic-update-slice | bytes 110596 | tf_op jit(solution)/shard_map/while/body/eval_jaxpr/dynamic_update_slice | solution.py:124
  319.0 16.8 %dynamic_update_slice.27 = f32[48,48,152]{2,1,0:T(8,128)S(1)} dynamic-update-slice(f32[48,48,152]{2,1,0:T(8,128)S(1)} %get-tuple-element.505, f32[24,24,24]{2,1,0:T(8,128)S(1)} %dynamic-slice_add_fusion.4, s32[]{:T(128)S(6)} %select_n.230, s32[]{:T(128)S(6)} %select_n.231, s32[]{:T(128)S(6)} %select_n.232) | dynamic-update-slice | bytes 110596 | tf_op jit(solution)/shard_map/while/body/eval_jaxpr/dynamic_update_slice | solution.py:124
  341.8 16.8 %dynamic_update_slice.28 = f32[48,48,152]{2,1,0:T(8,128)S(1)} dynamic-update-slice(f32[48,48,152]{2,1,0:T(8,128)S(1)} %dynamic_update_slice.27, f32[24,24,24]{2,1,0:T(8,128)S(1)} %dynamic-slice_add_fusion.5, s32[]{:T(128)S(6)} %select_n.233, s32[]{:T(128)S(6)} %select_n.234, s32[]{:T(128)S(6)} %select_n.235) | dynamic-update-slice | bytes 110596 | tf_op jit(solution)/shard_map/while/body/eval_jaxpr/dynamic_update_slice | solution.py:124
  366.4 22.1 %dynamic_update_slice.27 = f32[48,48,152]{2,1,0:T(8,128)S(1)} dynamic-update-slice(f32[48,48,152]{2,1,0:T(8,128)S(1)} %get-tuple-element.505, f32[24,24,24]{2,1,0:T(8,128)S(1)} %dynamic-slice_add_fusion.4, s32[]{:T(128)S(6)} %select_n.230, s32[]{:T(128)S(6)} %select_n.231, s32[]{:T(128)S(6)} %select_n.232) | dynamic-update-slice | bytes 110596 | tf_op jit(solution)/shard_map/while/body/eval_jaxpr/dynamic_update_slice | solution.py:124
  394.6 16.8 %dynamic_update_slice.28 = f32[48,48,152]{2,1,0:T(8,128)S(1)} dynamic-update-slice(f32[48,48,152]{2,1,0:T(8,128)S(1)} %dynamic_update_slice.27, f32[24,24,24]{2,1,0:T(8,128)S(1)} %dynamic-slice_add_fusion.5, s32[]{:T(128)S(6)} %select_n.233, s32[]{:T(128)S(6)} %select_n.234, s32[]{:T(128)S(6)} %select_n.235) | dynamic-update-slice | bytes 110596 | tf_op jit(solution)/shard_map/while/body/eval_jaxpr/dynamic_update_slice | solution.py:124
  419.1 21.6 %dynamic_update_slice.27 = f32[48,48,152]{2,1,0:T(8,128)S(1)} dynamic-update-slice(f32[48,48,152]{2,1,0:T(8,128)S(1)} %get-tuple-element.505, f32[24,24,24]{2,1,0:T(8,128)S(1)} %dynamic-slice_add_fusion.4, s32[]{:T(128)S(6)} %select_n.230, s32[]{:T(128)S(6)} %select_n.231, s32[]{:T(128)S(6)} %select_n.232) | dynamic-update-slice | bytes 110596 | tf_op jit(solution)/shard_map/while/body/eval_jaxpr/dynamic_update_slice | solution.py:124
  446.8 19.7 %dynamic_update_slice.28 = f32[48,48,152]{2,1,0:T(8,128)S(1)} dynamic-update-slice(f32[48,48,152]{2,1,0:T(8,128)S(1)} %dynamic_update_slice.27, f32[24,24,24]{2,1,0:T(8,128)S(1)} %dynamic-slice_add_fusion.5, s32[]{:T(128)S(6)} %select_n.233, s32[]{:T(128)S(6)} %select_n.234, s32[]{:T(128)S(6)} %select_n.235) | dynamic-update-slice | bytes 110596 | tf_op jit(solution)/shard_map/while/body/eval_jaxpr/dynamic_update_slice | solution.py:124
  474.3 17.9 %dynamic_update_slice.27 = f32[48,48,152]{2,1,0:T(8,128)S(1)} dynamic-update-slice(f32[48,48,152]{2,1,0:T(8,128)S(1)} %get-tuple-element.505, f32[24,24,24]{2,1,0:T(8,128)S(1)} %dynamic-slice_add_fusion.4, s32[]{:T(128)S(6)} %select_n.230, s32[]{:T(128)S(6)} %select_n.231, s32[]{:T(128)S(6)} %select_n.232) | dynamic-update-slice | bytes 110596 | tf_op jit(solution)/shard_map/while/body/eval_jaxpr/dynamic_update_slice | solution.py:124
  498.3 19.5 %dynamic_update_slice.28 = f32[48,48,152]{2,1,0:T(8,128)S(1)} dynamic-update-slice(f32[48,48,152]{2,1,0:T(8,128)S(1)} %dynamic_update_slice.27, f32[24,24,24]{2,1,0:T(8,128)S(1)} %dynamic-slice_add_fusion.5, s32[]{:T(128)S(6)} %select_n.233, s32[]{:T(128)S(6)} %select_n.234, s32[]{:T(128)S(6)} %select_n.235) | dynamic-update-slice | bytes 110596 | tf_op jit(solution)/shard_map/while/body/eval_jaxpr/dynamic_update_slice | solution.py:124
  525.5 18.6 %dynamic_update_slice.27 = f32[48,48,152]{2,1,0:T(8,128)S(1)} dynamic-update-slice(f32[48,48,152]{2,1,0:T(8,128)S(1)} %get-tuple-element.505, f32[24,24,24]{2,1,0:T(8,128)S(1)} %dynamic-slice_add_fusion.4, s32[]{:T(128)S(6)} %select_n.230, s32[]{:T(128)S(6)} %select_n.231, s32[]{:T(128)S(6)} %select_n.232) | dynamic-update-slice | bytes 110596 | tf_op jit(solution)/shard_map/while/body/eval_jaxpr/dynamic_update_slice | solution.py:124
  550.2 16.8 %dynamic_update_slice.28 = f32[48,48,152]{2,1,0:T(8,128)S(1)} dynamic-update-slice(f32[48,48,152]{2,1,0:T(8,128)S(1)} %dynamic_update_slice.27, f32[24,24,24]{2,1,0:T(8,128)S(1)} %dynamic-slice_add_fusion.5, s32[]{:T(128)S(6)} %select_n.233, s32[]{:T(128)S(6)} %select_n.234, s32[]{:T(128)S(6)} %select_n.235) | dynamic-update-slice | bytes 110596 | tf_op jit(solution)/shard_map/while/body/eval_jaxpr/dynamic_update_slice | solution.py:124
  574.8 19.4 %dynamic_update_slice.27 = f32[48,48,152]{2,1,0:T(8,128)S(1)} dynamic-update-slice(f32[48,48,152]{2,1,0:T(8,128)S(1)} %get-tuple-element.505, f32[24,24,24]{2,1,0:T(8,128)S(1)} %dynamic-slice_add_fusion.4, s32[]{:T(128)S(6)} %select_n.230, s32[]{:T(128)S(6)} %select_n.231, s32[]{:T(128)S(6)} %select_n.232) | dynamic-update-slice | bytes 110596 | tf_op jit(solution)/shard_map/while/body/eval_jaxpr/dynamic_update_slice | solution.py:124
  600.3 16.8 %dynamic_update_slice.28 = f32[48,48,152]{2,1,0:T(8,128)S(1)} dynamic-update-slice(f32[48,48,152]{2,1,0:T(8,128)S(1)} %dynamic_update_slice.27, f32[24,24,24]{2,1,0:T(8,128)S(1)} %dynamic-slice_add_fusion.5, s32[]{:T(128)S(6)} %select_n.233, s32[]{:T(128)S(6)} %select_n.234, s32[]{:T(128)S(6)} %select_n.235) | dynamic-update-slice | bytes 110596 | tf_op jit(solution)/shard_map/while/body/eval_jaxpr/dynamic_update_slice | solution.py:124
  624.9 18.9 %dynamic_update_slice.27 = f32[48,48,152]{2,1,0:T(8,128)S(1)} dynamic-update-slice(f32[48,48,152]{2,1,0:T(8,128)S(1)} %get-tuple-element.505, f32[24,24,24]{2,1,0:T(8,128)S(1)} %dynamic-slice_add_fusion.4, s32[]{:T(128)S(6)} %select_n.230, s32[]{:T(128)S(6)} %select_n.231, s32[]{:T(128)S(6)} %select_n.232) | dynamic-update-slice | bytes 110596 | tf_op jit(solution)/shard_map/while/body/eval_jaxpr/dynamic_update_slice | solution.py:124
  649.9 16.8 %dynamic_update_slice.28 = f32[48,48,152]{2,1,0:T(8,128)S(1)} dynamic-update-slice(f32[48,48,152]{2,1,0:T(8,128)S(1)} %dynamic_update_slice.27, f32[24,24,24]{2,1,0:T(8,128)S(1)} %dynamic-slice_add_fusion.5, s32[]{:T(128)S(6)} %select_n.233, s32[]{:T(128)S(6)} %select_n.234, s32[]{:T(128)S(6)} %select_n.235) | dynamic-update-slice | bytes 110596 | tf_op jit(solution)/shard_map/while/body/eval_jaxpr/dynamic_update_slice | solution.py:124
  674.4 11.6 dynamic_update_slice.27
  692.2 16.8 %dynamic_update_slice.28 = f32[48,48,152]{2,1,0:T(8,128)S(1)} dynamic-update-slice(f32[48,48,152]{2,1,0:T(8,128)S(1)} %dynamic_update_slice.27, f32[24,24,24]{2,1,0:T(8,128)S(1)} %dynamic-slice_add_fusion.5, s32[]{:T(128)S(6)} %select_n.233, s32[]{:T(128)S(6)} %select_n.234, s32[]{:T(128)S(6)} %select_n.235) | dynamic-update-slice | bytes 110596 | tf_op jit(solution)/shard_map/while/body/eval_jaxpr/dynamic_update_slice | solution.py:124
  716.7 19.7 %dynamic_update_slice.27 = f32[48,48,152]{2,1,0:T(8,128)S(1)} dynamic-update-slice(f32[48,48,152]{2,1,0:T(8,128)S(1)} %get-tuple-element.505, f32[24,24,24]{2,1,0:T(8,128)S(1)} %dynamic-slice_add_fusion.4, s32[]{:T(128)S(6)} %select_n.230, s32[]{:T(128)S(6)} %select_n.231, s32[]{:T(128)S(6)} %select_n.232) | dynamic-update-slice | bytes 110596 | tf_op jit(solution)/shard_map/while/body/eval_jaxpr/dynamic_update_slice | solution.py:124
  742.6 19.7 %dynamic_update_slice.28 = f32[48,48,152]{2,1,0:T(8,128)S(1)} dynamic-update-slice(f32[48,48,152]{2,1,0:T(8,128)S(1)} %dynamic_update_slice.27, f32[24,24,24]{2,1,0:T(8,128)S(1)} %dynamic-slice_add_fusion.5, s32[]{:T(128)S(6)} %select_n.233, s32[]{:T(128)S(6)} %select_n.234, s32[]{:T(128)S(6)} %select_n.235) | dynamic-update-slice | bytes 110596 | tf_op jit(solution)/shard_map/while/body/eval_jaxpr/dynamic_update_slice | solution.py:124
  770.1 20.5 %dynamic_update_slice.27 = f32[48,48,152]{2,1,0:T(8,128)S(1)} dynamic-update-slice(f32[48,48,152]{2,1,0:T(8,128)S(1)} %get-tuple-element.505, f32[24,24,24]{2,1,0:T(8,128)S(1)} %dynamic-slice_add_fusion.4, s32[]{:T(128)S(6)} %select_n.230, s32[]{:T(128)S(6)} %select_n.231, s32[]{:T(128)S(6)} %select_n.232) | dynamic-update-slice | bytes 110596 | tf_op jit(solution)/shard_map/while/body/eval_jaxpr/dynamic_update_slice | solution.py:124
  796.6 18.5 %dynamic_update_slice.28 = f32[48,48,152]{2,1,0:T(8,128)S(1)} dynamic-update-slice(f32[48,48,152]{2,1,0:T(8,128)S(1)} %dynamic_update_slice.27, f32[24,24,24]{2,1,0:T(8,128)S(1)} %dynamic-slice_add_fusion.5, s32[]{:T(128)S(6)} %select_n.233, s32[]{:T(128)S(6)} %select_n.234, s32[]{:T(128)S(6)} %select_n.235) | dynamic-update-slice | bytes 110596 | tf_op jit(solution)/shard_map/while/body/eval_jaxpr/dynamic_update_slice | solution.py:124
  822.9 18.1 %dynamic_update_slice.27 = f32[48,48,152]{2,1,0:T(8,128)S(1)} dynamic-update-slice(f32[48,48,152]{2,1,0:T(8,128)S(1)} %get-tuple-element.505, f32[24,24,24]{2,1,0:T(8,128)S(1)} %dynamic-slice_add_fusion.4, s32[]{:T(128)S(6)} %select_n.230, s32[]{:T(128)S(6)} %select_n.231, s32[]{:T(128)S(6)} %select_n.232) | dynamic-update-slice | bytes 110596 | tf_op jit(solution)/shard_map/while/body/eval_jaxpr/dynamic_update_slice | solution.py:124
  847.1 19.9 %dynamic_update_slice.28 = f32[48,48,152]{2,1,0:T(8,128)S(1)} dynamic-update-slice(f32[48,48,152]{2,1,0:T(8,128)S(1)} %dynamic_update_slice.27, f32[24,24,24]{2,1,0:T(8,128)S(1)} %dynamic-slice_add_fusion.5, s32[]{:T(128)S(6)} %select_n.233, s32[]{:T(128)S(6)} %select_n.234, s32[]{:T(128)S(6)} %select_n.235) | dynamic-update-slice | bytes 110596 | tf_op jit(solution)/shard_map/while/body/eval_jaxpr/dynamic_update_slice | solution.py:124
  868.4 6.9 scatter-add.4
  881.2 4.0 collective-permute-start.1
  885.3 3.6 collective-permute-done.1
  889.0 14.3 %all-gather = bf16[48,24,128]{2,1,0:T(8,128)(2,1)S(1)} all-gather(bf16[24,24,128]{2,1,0:T(8,128)(2,1)S(1)} %fusion.68), channel_id=2, replica_groups=mesh['gz'=16,'gy'=8,'orb'=2] {'orb'}, dimensions={0}, use_global_device_ids=true | all-gather | bytes 442368 | tf_op jit(solution)/shard_map/all_gather | solution.py:135
  903.3 4.2 collective-permute-start.2
  907.5 15.5 %collective-permute-start.3 = (bf16[6,24,128]{2,1,0:T(8,128)(2,1)S(1)}, bf16[6,24,128]{2,1,0:T(8,128)(2,1)S(1)}, u32[]{:S(2)}, u32[]{:S(2)}) collective-permute-start(bf16[6,24,128]{2,1,0:T(8,128)(2,1)S(1)} %get-tuple-element.319), channel_id=1, source_target_pairs={{16,0},{32,16},{48,32},{64,48},{80,64},{96,80},{112,96},{128,112},... | collective-permute-start | bytes 110600 | tf_op jit(solution)/shard_map/ppermute | solution.py:31
  924.0 4.0 collective-permute-start.4
  927.9 6.6 collective-permute-start.5
  936.2 3.1 fusion.33
  939.3 4.9 fusion.23
  944.2 3.4 fusion.26
  950.4 77.4 %while.39 = (s32[]{:T(128)}, bf16[6,12288]{1,0:T(8,128)(2,1)S(1)}, f32[6,8,12288]{2,0,1:T(8,128)}, f32[8,64]{1,0:T(8,128)S(1)}, f32[64]{0:T(128)S(1)}, /*index=5...) while((s32[]{:T(128)}, bf16[6,12288]{1,0:T(8,128)(2,1)S(1)}, ...), condition=%wide.region_6.7_spmd, body=%wide.region_5.6_spmd.sunk | while | flops 696791040 | bytes 14027641 | solution.py:80
  952.7 2.7 fusion.164
  955.4 3.8 fusion.165
  965.6 2.7 fusion.164
  968.3 3.8 fusion.165
  978.5 2.7 fusion.164
  981.2 3.8 fusion.165
  991.4 2.7 fusion.164
  994.1 3.8 fusion.165
  1004.3 2.7 fusion.164
  1007.0 3.8 fusion.165
  1017.2 2.7 fusion.164
  1019.8 3.8 fusion.165
  1028.0 26.2 %collective-permute-start.6 = (bf16[24,24,128]{2,1,0:T(8,128)(2,1)S(1)}, bf16[24,24,128]{2,1,0:T(8,128)(2,1)S(1)}, u32[]{:S(2)}, u32[]{:S(2)}) collective-permute-start(bf16[24,24,128]{2,1,0:T(8,128)(2,1)S(1)} %convert_element_type.310), channel_id=1, source_target_pairs={{0,14},{2,0},{4,2},{6,4},{8,6},{10,8},{12,10},{14,12},{1,15},{3,1}... | collective-permute-start | bytes 442376 | tf_op jit(solution)/shard_map/ppermute | solution.py:19
  1056.3 6.2 collective-permute-start.7
  1063.8 211.3 %while.40 = (s32[]{:T(128)}, bf16[16,2,13824]{2,1,0:T(2,128)(2,1)S(1)}, s32[16,2,3]{2,1,0:T(2,128)}, bf16[48,48,152]{2,1,0:T(8,128)(2,1)S(1)}, s32[]{:T(128)}, /*index=5*/s32[]{:T(128)}, s32[]{:T(128)}, s32[]{:T(128)}) while((s32[]{:T(128)}, bf16[16,2,13824]{2,1,0:T(2,128)(2,1)S(1)}, s32[16,2,3]{2,1,0:T(2,128)}, ...), condition=%wide.region_8.9_spmd, body=%wide.region_7.8_spmd.sunk | while | flops 110612 | bytes 387489 | solution.py:157
  1275.2 32.9 %all_to_all.15 = bf16[16,2,13824]{2,1,0:T(2,128)(2,1)S(1)} all-to-all(bf16[16,2,13824]{2,1,0:T(2,128)(2,1)S(1)} %get-tuple-element.204), channel_id=1, replica_groups=mesh['gz'=16,'gy'=8,'orb'=2] {'gz'}, dimensions={0} | all-to-all | bytes 1769472 | tf_op jit(solution)/shard_map/all_to_all | solution.py:160
  (331 shorter events, 149.6 us)
Async XLA Ops:
  3.9 16.9 %all-to-all-start = ((bf16[16,2,3]{2,1,0:T(2,128)(2,1)}), bf16[16,2,3]{2,1,0:T(2,128)(2,1)S(1)}, u32[]{:S(2)}, u32[]{:S(2)}) async-start(bf16[16,2,3]{2,1,0:T(2,128)(2,1)} %bitcast.41), calls=%async_computation | async-start | bytes 16384 | tf_op jit(solution)/shard_map/all_to_all | solution.py:109
  15.8 10.6 copy-start.22
  20.8 29.7 %all-to-all-start.1 = ((bf16[16,2,13824]{2,1,0:T(2,128)(2,1)}), bf16[16,2,13824]{2,1,0:T(2,128)(2,1)}, u32[]{:S(2)}, u32[]{:S(2)}) async-start(bf16[16,2,13824]{2,1,0:T(2,128)(2,1)} %reshape.511), calls=%async_computation.1 | async-start | bytes 1769472 | tf_op jit(solution)/shard_map/all_to_all | solution.py:106
  31.3 19.5 %copy-start.19 = (s32[16,2,3]{2,1,0:T(2,128)}, s32[16,2,3]{2,1,0:T(2,128)S(1)}, u32[]{:S(2)}) copy-start(s32[16,2,3]{2,1,0:T(2,128)S(1)} %convert_convert_fusion) | copy-start | bytes 1156
  868.3 67.8 %copy-start.2 = (f32[128,128]{1,0:T(8,128)S(1)}, f32[128,128]{1,0:T(8,128)}, u32[]{:S(2)}) copy-start(f32[128,128]{1,0:T(8,128)} %compare_convert_fusion.12) | copy-start | bytes 196612
  868.3 67.7 %copy-start.3 = (f32[128,128]{1,0:T(8,128)S(1)}, f32[128,128]{1,0:T(8,128)}, u32[]{:S(2)}) copy-start(f32[128,128]{1,0:T(8,128)} %get-tuple-element.335) | copy-start | bytes 196612
  868.3 67.7 %copy-start.4 = (f32[128,128]{1,0:T(8,128)S(1)}, f32[128,128]{1,0:T(8,128)}, u32[]{:S(2)}) copy-start(f32[128,128]{1,0:T(8,128)} %get-tuple-element.336) | copy-start | bytes 196612
  868.3 67.7 %copy-start.5 = (f32[128,128]{1,0:T(8,128)S(1)}, f32[128,128]{1,0:T(8,128)}, u32[]{:S(2)}) copy-start(f32[128,128]{1,0:T(8,128)} %get-tuple-element.337) | copy-start | bytes 196612
  868.3 67.7 %copy-start.6 = (f32[128,128]{1,0:T(8,128)S(1)}, f32[128,128]{1,0:T(8,128)}, u32[]{:S(2)}) copy-start(f32[128,128]{1,0:T(8,128)} %get-tuple-element.338) | copy-start | bytes 196612
  868.3 67.7 %copy-start.7 = (f32[128,128]{1,0:T(8,128)S(1)}, f32[128,128]{1,0:T(8,128)}, u32[]{:S(2)}) copy-start(f32[128,128]{1,0:T(8,128)} %get-tuple-element.339) | copy-start | bytes 196612
  868.3 67.7 %copy-start.8 = (f32[128,128]{1,0:T(8,128)S(1)}, f32[128,128]{1,0:T(8,128)}, u32[]{:S(2)}) copy-start(f32[128,128]{1,0:T(8,128)} %get-tuple-element.340) | copy-start | bytes 196612
  868.3 67.7 %copy-start.9 = (f32[128,128]{1,0:T(8,128)S(1)}, f32[128,128]{1,0:T(8,128)}, u32[]{:S(2)}) copy-start(f32[128,128]{1,0:T(8,128)} %get-tuple-element.341) | copy-start | bytes 196612
  868.3 67.7 %copy-start.10 = (f32[128,128]{1,0:T(8,128)S(1)}, f32[128,128]{1,0:T(8,128)}, u32[]{:S(2)}) copy-start(f32[128,128]{1,0:T(8,128)} %get-tuple-element.342) | copy-start | bytes 196612
  868.4 67.7 %copy-start.11 = (f32[128,128]{1,0:T(8,128)S(1)}, f32[128,128]{1,0:T(8,128)}, u32[]{:S(2)}) copy-start(f32[128,128]{1,0:T(8,128)} %get-tuple-element.343) | copy-start | bytes 196612
  868.4 67.7 %copy-start.12 = (f32[128,128]{1,0:T(8,128)S(1)}, f32[128,128]{1,0:T(8,128)}, u32[]{:S(2)}) copy-start(f32[128,128]{1,0:T(8,128)} %get-tuple-element.344) | copy-start | bytes 196612
  876.4 3.7 collective-permute-start
  881.2 7.7 collective-permute-start.1
  903.3 20.5 %collective-permute-start.2 = (bf16[6,24,128]{2,1,0:T(8,128)(2,1)S(1)}, bf16[6,24,128]{2,1,0:T(8,128)(2,1)S(1)}, u32[]{:S(2)}, u32[]{:S(2)}) collective-permute-start(bf16[6,24,128]{2,1,0:T(8,128)(2,1)S(1)} %get-tuple-element.318), channel_id=1, source_target_pairs={{0,16},{16,32},{32,48},{48,64},{64,80},{80,96},{96,112},{112,128},... | collective-permute-start | bytes 110600 | tf_op jit(solution)/shard_map/ppermute | solution.py:29
  907.5 16.4 %collective-permute-start.3 = (bf16[6,24,128]{2,1,0:T(8,128)(2,1)S(1)}, bf16[6,24,128]{2,1,0:T(8,128)(2,1)S(1)}, u32[]{:S(2)}, u32[]{:S(2)}) collective-permute-start(bf16[6,24,128]{2,1,0:T(8,128)(2,1)S(1)} %get-tuple-element.319), channel_id=1, source_target_pairs={{16,0},{32,16},{48,32},{64,48},{80,64},{96,80},{112,96},{128,112},... | collective-permute-start | bytes 110600 | tf_op jit(solution)/shard_map/ppermute | solution.py:31
  924.0 12.0 collective-permute-start.4
  927.9 8.1 collective-permute-start.5
  936.1 3.2 copy-start.13
  936.1 3.2 copy-start.14
  936.1 3.2 copy-start.15
  936.1 3.2 copy-start.16
  936.2 3.2 copy-start.17
  948.1 2.3 copy-start.18
  948.1 2.3 copy-start.20
  948.1 2.2 copy-start.21
  948.1 2.2 copy-start.23
  948.1 2.2 copy-start.24
  1028.0 35.8 %copy-start.1 = (bf16[24,24,128]{2,1,0:T(8,128)(2,1)}, bf16[24,24,128]{2,1,0:T(8,128)(2,1)S(1)}, u32[]{:S(2)}) copy-start(bf16[24,24,128]{2,1,0:T(8,128)(2,1)S(1)} %convert_element_type.310) | copy-start | bytes 442372
  1028.0 28.3 %collective-permute-start.6 = (bf16[24,24,128]{2,1,0:T(8,128)(2,1)S(1)}, bf16[24,24,128]{2,1,0:T(8,128)(2,1)S(1)}, u32[]{:S(2)}, u32[]{:S(2)}) collective-permute-start(bf16[24,24,128]{2,1,0:T(8,128)(2,1)S(1)} %convert_element_type.310), channel_id=1, source_target_pairs={{0,14},{2,0},{4,2},{6,4},{8,6},{10,8},{12,10},{14,12},{1,15},{3,1}... | collective-permute-start | bytes 442376 | tf_op jit(solution)/shard_map/ppermute | solution.py:19
  1056.3 7.4 collective-permute-start.7
  1275.2 34.0 %copy-start = (bf16[16,24,576]{2,1,0:T(8,128)(2,1)S(1)}, bf16[16,24,576]{2,1,0:T(8,128)(2,1)}, u32[]{:S(2)}) copy-start(bf16[16,24,576]{2,1,0:T(8,128)(2,1)} %param.26) | copy-start | bytes 1327108
